TPU v7x, 32 devices: a whole 2x2x4 slice. The times are simulated.
32 devices in a mesh: row: 4 (over y, x), col: 2 (over core), depth: 4 (over z).
Axes of the slice: x: 2, y: 2, z: 4, core: 2. Of those that a mesh axis runs over, the one named last changes fastest.
Arguments:
- integrals: float32 [8, 6144, 4096], P(('col', 'depth'), 'row'), may hold values from -0.0546875 to 0.0546875
- amplitudes: float32 [8, 256, 4096], P('col', ('row', 'depth')), may hold values from -6 to 6
- block_list: int32 [8, 4], P('col'), may hold values from -1 to 7, as said below
- pair_list: int32 [256, 2], replicated, may hold values from 0 to 15, as said below
Outputs:
- residual: float32 [256, 6144], P(None, ('row', 'col', 'depth'))
Inputs may be any that keep to these rules, and one draw needn't show every extreme that they name: `block_list`: slot s belongs to summation index s // 4; a live entry names a column block b with b // 4 equal to that index. The live slots of one row block and one summation index name distinct blocks, between 2 and 4 of them, lying anywhere among its 4 slots; in every draw some row block and index have exactly 4. `pair_list`: the rows are all 16 x 16 ordered pairs (i, j), each once, in a drawn order.
All inputs are finite; a program needn't handle non-finite values.
Results may differ from a plain program's by a relative error of at most 0.0003.
Values sent between devices are 32-bit elements; how exact they have to be, the bound alone decides.
A program may use at most 128 MiB of HBM per device.

v0:
```python
import jax
import jax.numpy as jnp
from jax import lax
from jax.sharding import PartitionSpec as P

NOCC = 16


def slot_product(chosen, slab_rows):
    return lax.dot_general(
        chosen,
        slab_rows,
        (((1,), (1,)), ((), ())),
        precision=lax.Precision.HIGHEST,
        preferred_element_type=jnp.float32,
    )


def add_slots(amp_part, slab, slot_ids):
    blocks_here = amp_part.shape[0]
    ident = slot_ids[0]
    living = ident >= 0
    locate = jnp.maximum(ident, 0) % blocks_here
    chosen = lax.dynamic_index_in_dim(amp_part, locate, 0, keepdims=False)
    slab_rows = slab[0]
    result = jnp.where(living, slot_product(chosen, slab_rows), jnp.zeros((), jnp.float32))
    return result


def per_device(integrals, amplitudes, block_list, pair_list):
    share_count = integrals.shape[0]
    first_slot = lax.axis_index("depth") * share_count
    row_ids = lax.dynamic_index_in_dim(block_list, lax.axis_index("row"), 1, keepdims=False)
    own_ids = lax.dynamic_slice_in_dim(row_ids, first_slot, share_count, 0)
    partial_value = add_slots(
        lax.all_gather(amplitudes, ("row", "depth"), axis=1, tiled=True), integrals, own_ids
    )
    shares = lax.psum_scatter(partial_value, ("col", "depth"), scatter_dimension=1, tiled=True)
    codes = pair_list[:, 0] * NOCC + pair_list[:, 1]
    mirror_codes = pair_list[:, 1] * NOCC + pair_list[:, 0]
    one_hot = (mirror_codes[:, None] == codes[None, :]).astype(jnp.float32)
    mirrored = jnp.dot(
        one_hot, shares, precision=lax.Precision.HIGHEST, preferred_element_type=jnp.float32
    )
    return shares + mirrored


def solution(mesh):
    return jax.shard_map(
        per_device,
        mesh=mesh,
        in_specs=(
            P(("col", "depth"), "row", None),
            P("col", ("row", "depth"), None),
            P("col", None),
            P(),
        ),
        out_specs=P(None, ("row", "col", "depth")),
        check_vma=False,
    )
```

profile of v0, /device:TPU:1, one launch (start us, length us, event | category | flops | bytes accessed | tf_op | source)
XLA Modules:
  0.0 275.9 jit_solution(15797697840048514006)
XLA Ops:
  6.5 0.0 all-gather.2.cloned.1.call-start
  6.5 0.7 all-gather.2.cloned.1.call-update
  7.3 0.0 reduce-scatter.2.cloned.1.call-start
  7.3 1.3 dynamic_slice.9
  9.9 193.4 %all-gather.2.cloned.1.call-done = f32[4,256,4096]{2,1,0:T(8,128)} async-done(((f32[4,16,4096]{2,1,0:T(8,128)}), f32[4,256,4096]{2,1,0:T(8,128)}) %all-gather.2.cloned.1.call-update) | async-done | bytes 16777232 | tf_op jit(solution)/shard_map/all_gather | solution.py:36
  203.3 0.0 copy-start
  203.3 25.0 %fusion.4 = f32[256,1536]{0,1:T(8,128)} fusion(f32[1,1536,4096]{2,1,0:T(8,128)} %param.4, f32[4,256,4096]{2,1,0:T(8,128)} %all-gather.2.cloned.1.call-done, s32[]{:T(128)S(6)} %select_n.36, pred[]{:T(512)} %bitcast), kind=kOutput, calls=%fused_computation.4 | convolution fusion | flops 19327746048 | bytes 30933508 | tf_op jit(solution)/shard_map/dot_general | solution.py:10
  228.3 0.0 reduce-scatter.2.cloned.1.call-update
  228.3 0.0 copy-done
  228.3 38.6 %reduce-scatter.2.cloned.1.call-done = f32[256,192]{0,1:T(8,128)} async-done(((f32[256,1536]{0,1:T(8,128)}), f32[256,192]{0,1:T(8,128)}) %reduce-scatter.2.cloned.1.call-update) | async-done | bytes 196624 | tf_op jit(solution)/shard_map/reduce_scatter | solution.py:38
  267.0 2.1 convolution_add_fusion
  (1 shorter events, 0.0 us)
Async XLA Ops:
  6.5 196.8 %all-gather.2.cloned.1.call-start = ((), (), s32[]{:S(2)}) async-start(), calls=%async_computation.1 | async-start | bytes 17825792 | tf_op jit(solution)/shard_map/all_gather | solution.py:36
  7.3 259.7 %reduce-scatter.2.cloned.1.call-start = ((), (), s32[]{:S(2)}) async-start(), calls=%async_computation.2 | async-start | bytes 1769472 | tf_op jit(solution)/shard_map/reduce_scatter | solution.py:38
  203.3 25.0 %copy-start = (s32[256,2]{0,1:T(2,128)S(1)}, s32[256,2]{0,1:T(2,128)}, u32[]{:S(2)}) copy-start(s32[256,2]{0,1:T(2,128)} %param.7) | copy-start | bytes 6148
Sparse Core Ops, SparseCore 0:
  10.2 193.0 all-gather.1
  228.4 38.4 reduce-scatter.1
where the time goes:
time: 276 us
  waiting for transfers between devices  233 us (84%)
  matrix products  27.1 us (10%)
  between operations  14.7 us (5%)
    all_gather x1, waiting for transfers between devices, per_device(): lax.all_gather(amplitudes, ('row', 'depth'), axis=1, tiled=True)  193 us
    reduce_scatter x1, waiting for transfers between devices, per_device(): lax.psum_scatter(partial_value, ('col', 'depth'), scatter_dimension=1, ti...  38.6 us
    dot_general x1, matrix products, slot_product(): lax.dot_general(chosen, slab_rows, (((1,), (1,)), ((), ())), precision=la...  25 us
  transfers between devices with their start and end apart: 2, of which 2 were waited for; matrix products, arithmetic and copies ran while one was open for 0% of the time, Pallas kernels for 0%

commit v1 on v0

v1 whole, which is shorter than its diff:
```python
import functools

import jax
import jax.numpy as jnp
from jax import lax
from jax.experimental import pallas as pl
from jax.experimental.pallas import tpu as pltpu
from jax.sharding import PartitionSpec as P

F32 = jnp.float32
BF16 = jnp.bfloat16
CHUNK = 128
NT = (((1,), (1,)), ((), ()))


def split2(value):
    high = value.astype(BF16)
    return high, (value - high.astype(F32)).astype(BF16)


def dot(lhs, rhs):
    return jnp.dot(lhs, rhs, preferred_element_type=F32)


def ladder_kernel(
    nr, nc, nd,
    codes_all, codes_plane, blocks, amp, integ, out,
    slab, raw, joint, staged, chosen, acc, got_col, got_depth, mask_in, mask_ext,
    slab_sem, first_send, first_recv, line_send, line_recv, plane_send, plane_recv,
    col_send, col_recv, depth_send, depth_recv,
):
    r = lax.axis_index("row")
    c = lax.axis_index("col")
    d = lax.axis_index("depth")
    nblk, own_pairs, width = amp.shape
    quarter = width // nr
    steps = quarter // CHUNK
    plane_pairs = nr * own_pairs
    sym = out.shape[0]
    share = out.shape[1]

    def remote(src, dst, send, recv, **to):
        return pltpu.make_async_remote_copy(
            src_ref=src, dst_ref=dst, send_sem=send, recv_sem=recv,
            device_id=to, device_id_type=pl.DeviceIdType.MESH,
        )

    inner = jnp.logical_and(d >= 1, d <= 2)
    outer = jnp.logical_or(d == 0, d == 3)
    lower = d < 2
    ext = jnp.where(lower, 0, 3)
    mate = 3 - d
    inward = jnp.where(lower, d + 1, d - 1)
    outward = jnp.where(lower, 0, 3)

    barrier = pltpu.get_barrier_semaphore()
    for o in range(1, nr):
        pl.semaphore_signal(barrier, inc=1, device_id={"row": lax.rem(r + o, nr)},
                            device_id_type=pl.DeviceIdType.MESH)
    for o in range(1, nc):
        pl.semaphore_signal(barrier, inc=1, device_id={"col": lax.rem(c + o, nc)},
                            device_id_type=pl.DeviceIdType.MESH)
    for o in range(1, nd):
        pl.semaphore_signal(barrier, inc=1, device_id={"depth": lax.rem(d + o, nd)},
                            device_id_type=pl.DeviceIdType.MESH)
    pl.semaphore_wait(barrier, nr + nc + nd - 3)

    def first_copy(j, o):
        to = lax.rem(r + o, nr)
        at = pl.multiple_of(to * quarter + j * CHUNK, CHUNK)
        src = amp.at[:, :, pl.ds(at, CHUNK)]
        dst = raw.at[j, d, :, pl.ds(pl.multiple_of(r * own_pairs, own_pairs), own_pairs), :]
        if o == 0:
            return pltpu.make_async_copy(src, dst, first_recv.at[j, 0])
        return remote(src, dst, first_send.at[j, o], first_recv.at[j, o], row=to)

    def first_start(j, _):
        for o in range(nr):
            first_copy(j, o).start()
        return 0

    lax.fori_loop(0, steps, first_start, 0)
    slab_copy = pltpu.make_async_copy(integ.at[0], slab, slab_sem)
    slab_copy.start()

    def one_hot(codes):
        n = codes.shape[1]
        at = lax.broadcasted_iota(jnp.int32, (sym, n), 0)
        return jnp.where((codes >> 2) == at, codes & 3, 0).astype(F32)

    plane_of = lax.broadcasted_iota(jnp.int32, (sym, nd * plane_pairs), 1) // plane_pairs
    mask_in[...] = jnp.where(plane_of == ext, 0.0, one_hot(codes_all[...]))
    mask_ext[...] = one_hot(codes_plane[ext])
    acc[...] = jnp.zeros_like(acc)

    def own_copy(j):
        return remote(raw.at[j, d], raw.at[j, d], line_send.at[j, 0], line_recv.at[j, d], depth=inward)

    def forward_copy(j):
        return remote(raw.at[j, outward], raw.at[j, outward], line_send.at[j, 1],
                      line_recv.at[j, outward], depth=inward)

    def joint_copy(j):
        return remote(joint.at[j], joint.at[j], line_send.at[j, 2], line_recv.at[j, nd], depth=outward)

    def raw_arrived(j, z):
        remote(raw.at[j, z], raw.at[j, z], line_send.at[j, 0], line_recv.at[j, z], depth=inward).wait_recv()

    def plane_copy(j, o):
        to = lax.rem(r + o, nr)
        return remote(staged.at[j, o], chosen.at[j, r], plane_send.at[j, o], plane_recv.at[j, o], row=to)

    def spread(j):
        m_ext = mask_ext[...].astype(BF16)
        sums = []
        for b in range(nblk):
            high, low = split2(raw[j, ext, b])
            sums.append(joint[j, b] + (dot(m_ext, high) + dot(m_ext, low)))
        for o in range(nr):
            to = lax.rem(r + o, nr)
            at = lax.rem(jnp.maximum(blocks[d, to], 0), nblk)
            picked = sums[0]
            for b in range(1, nblk):
                picked = jnp.where(at == b, sums[b], picked)
            if o == 0:
                chosen[j, r] = picked
            else:
                staged[j, o] = picked
                plane_copy(j, o).start()

    def step(t, _):
        @pl.when(t < steps)
        def _():
            for o in range(nr):
                copy = first_copy(t, o)
                if o == 0:
                    copy.wait()
                else:
                    copy.wait_recv()
            own_copy(t).start()

        @pl.when(jnp.logical_and(inner, jnp.logical_and(t >= 1, t < steps + 1)))
        def _():
            raw_arrived(t - 1, outward)
            forward_copy(t - 1).start()

        @pl.when(jnp.logical_and(inner, jnp.logical_and(t >= 2, t < steps + 2)))
        def _():
            j = t - 2
            raw_arrived(j, mate)
            raw_arrived(j, 3 - outward)
            m_in = mask_in[...].astype(BF16)
            for b in range(nblk):
                high, low = split2(raw[j, :, b].reshape(nd * plane_pairs, CHUNK))
                joint[j, b] = dot(m_in, high) + dot(m_in, low)
            joint_copy(j).start()
            spread(j)

        @pl.when(jnp.logical_and(outer, jnp.logical_and(t >= 3, t < steps + 3)))
        def _():
            joint_copy(t - 3).wait_recv()
            spread(t - 3)

        @pl.when(t == 4)
        def _():
            slab_copy.wait()

        @pl.when(t >= 4)
        def _():
            j = t - 4
            for o in range(1, nr):
                plane_copy(j, o).wait_recv()
            lhs = jnp.concatenate([chosen[j, q] for q in range(nr)], axis=1)
            l_high, l_low = split2(lhs)

            def tile(s, _):
                rows = pl.ds(pl.multiple_of(s * share, 8), share)
                rhs = jnp.concatenate(
                    [slab[rows, pl.ds(pl.multiple_of(q * quarter + j * CHUNK, CHUNK), CHUNK)]
                     for q in range(nr)], axis=1)
                r_high, r_low = split2(rhs)
                value = lax.dot_general(l_high, r_high, NT, preferred_element_type=F32)
                value += lax.dot_general(l_high, r_low, NT, preferred_element_type=F32)
                value += lax.dot_general(l_low, r_high, NT, preferred_element_type=F32)
                acc[s // nd, lax.rem(s, nd)] += value
                return 0

            lax.fori_loop(0, nc * nd, tile, 0)

        return 0

    lax.fori_loop(0, steps + 4, step, 0)

    live = blocks[d, r] >= 0
    acc[...] = jnp.where(live, acc[...], 0.0)

    def col_copy(o):
        to = lax.rem(c + o, nc)
        return remote(acc.at[to], got_col.at[o], col_send.at[o], col_recv.at[o], col=to)

    for o in range(1, nc):
        col_copy(o).start()
    for o in range(1, nc):
        col_copy(o).wait_recv()
    total = acc[c]
    for o in range(1, nc):
        total += got_col[o]
    got_col[0] = total

    def depth_copy(o):
        to = lax.rem(d + o, nd)
        return remote(got_col.at[0, to], got_depth.at[o], depth_send.at[o], depth_recv.at[o], depth=to)

    for o in range(1, nd):
        depth_copy(o).start()
    for o in range(1, nd):
        depth_copy(o).wait_recv()
    total = got_col[0, d]
    for o in range(1, nd):
        total += got_depth[o]
    out[...] = total

    for o in range(1, nc):
        col_copy(o).wait_send()
    for o in range(1, nd):
        depth_copy(o).wait_send()

    def finish(j, _):
        for o in range(1, nr):
            first_copy(j, o).wait_send()
            plane_copy(j, o).wait_send()
        own_copy(j).wait_send()

        @pl.when(inner)
        def _():
            forward_copy(j).wait_send()
            joint_copy(j).wait_send()

        return 0

    lax.fori_loop(0, steps, finish, 0)


def per_device(mesh, integrals, amplitudes, block_list, pair_list):
    nr, nc, nd = mesh.shape["row"], mesh.shape["col"], mesh.shape["depth"]
    _, rows, width = integrals.shape
    nblk, own_pairs, _ = amplitudes.shape
    pairs = pair_list.shape[0]
    nocc = int(round(pairs ** 0.5))
    sym = nocc * (nocc + 1) // 2
    plane_pairs = nr * own_pairs
    share = rows // (nc * nd)
    steps = width // nr // CHUNK

    big = jnp.maximum(pair_list[:, 0], pair_list[:, 1])
    small = jnp.minimum(pair_list[:, 0], pair_list[:, 1])
    unordered = big * (big + 1) // 2 + small
    codes = unordered * 4 + jnp.where(big == small, 2, 1)
    codes = codes.reshape(nr, nd, own_pairs).transpose(1, 0, 2)
    codes_plane = codes.reshape(nd, 1, plane_pairs)
    codes_all = codes.reshape(1, pairs)

    dma = pltpu.SemaphoreType.DMA
    sums = pl.pallas_call(
        functools.partial(ladder_kernel, nr, nc, nd),
        out_shape=jax.ShapeDtypeStruct((sym, share), F32),
        in_specs=[
            pl.BlockSpec(memory_space=pltpu.VMEM),
            pl.BlockSpec(memory_space=pltpu.VMEM),
            pl.BlockSpec(memory_space=pltpu.SMEM),
            pl.BlockSpec(memory_space=pl.ANY),
            pl.BlockSpec(memory_space=pl.ANY),
        ],
        out_specs=pl.BlockSpec(memory_space=pltpu.VMEM),
        scratch_shapes=[
            pltpu.VMEM((rows, width), F32),
            pltpu.VMEM((steps, nd, nblk, plane_pairs, CHUNK), F32),
            pltpu.VMEM((steps, nblk, sym, CHUNK), F32),
            pltpu.VMEM((steps, nr, sym, CHUNK), F32),
            pltpu.VMEM((steps, nr, sym, CHUNK), F32),
            pltpu.VMEM((nc, nd, sym, share), F32),
            pltpu.VMEM((nc, nd, sym, share), F32),
            pltpu.VMEM((nd, sym, share), F32),
            pltpu.VMEM((sym, pairs), F32),
            pltpu.VMEM((sym, plane_pairs), F32),
            dma, dma((steps, nr)), dma((steps, nr)),
            dma((steps, 3)), dma((steps, nd + 1)),
            dma((steps, nr)), dma((steps, nr)),
            dma((nc,)), dma((nc,)), dma((nd,)), dma((nd,)),
        ],
        compiler_params=pltpu.CompilerParams(
            collective_id=0, has_side_effects=True, vmem_limit_bytes=56 * 1024 * 1024
        ),
        cost_estimate=pl.CostEstimate(
            flops=6 * sym * rows * width, bytes_accessed=4 * rows * width, transcendentals=0
        ),
    )(codes_all, codes_plane, block_list, amplitudes, integrals)

    expand = (unordered[:, None] == jnp.arange(sym)[None, :]).astype(F32)
    return jnp.dot(expand, sums, precision=lax.Precision.HIGHEST, preferred_element_type=F32)


def solution(mesh):
    return jax.shard_map(
        functools.partial(per_device, mesh),
        mesh=mesh,
        in_specs=(
            P(("col", "depth"), "row", None),
            P("col", ("row", "depth"), None),
            P("col", None),
            P(),
        ),
        out_specs=P(None, ("row", "col", "depth")),
        check_vma=False,
    )
```

time: 276 us -> 93.6 us (0.34)
  waiting for transfers between devices: 233 us -> 0 us
  Pallas kernels: 0 us -> 89.1 us
  matrix products: 27.1 us -> 1.99 us
  between operations: 14.7 us -> 0.02 us
    all_gather x1 -> x0, waiting for transfers between devices: 193 us -> none  [per_device(): lax.all_gather(amplitudes, ('row', 'depth'), axis=1, tiled=True)]
    pallas_call x0 -> x1, Pallas kernels: none -> 89.1 us  [per_device(): pl.pallas_call(functools.partial(ladder_kernel, nr, nc, nd), out_shape=ja...]
    reduce_scatter x1 -> x0, waiting for transfers between devices: 38.6 us -> none  [per_device(): lax.psum_scatter(partial_value, ('col', 'depth'), scatter_dimension=1, ti...]
    dot_general x2 -> x1, matrix products: 27.1 us -> 1.99 us  [per_device(): jnp.dot(expand, sums, precision=lax.Precision.HIGHEST, preferred_element_...]
  transfers between devices with their start and end apart: 2 -> 0, of which waited for: 2 -> 0; matrix products, arithmetic and copies ran while one was open for 0% -> 0% of each run, Pallas kernels for 0% -> 0%
where the time goes in v1:
time: 93.6 us; the launch traced here: 93.4 us
  Pallas kernels  89.1 us (95%)
  matrix products  1.99 us (2%)
  local copies, waits for them, and re-layouts  1.5 us (2%)
    pallas_call x1, Pallas kernels, per_device(): pl.pallas_call(functools.partial(ladder_kernel, nr, nc, nd), out_shape=ja...  89.1 us
    dot_general x1, matrix products, per_device(): jnp.dot(expand, sums, precision=lax.Precision.HIGHEST, preferred_element_...  1.99 us

profile of v1, /device:TPU:1, one launch (start us, length us, event | category | flops | bytes accessed | tf_op | source)
XLA Modules:
  0.0 93.4 jit_solution(15389333705048396043)
XLA Ops:
  0.0 0.8 fusion.9
  0.8 0.1 max.9
  0.9 0.1 min.9
  1.0 0.7 reshape.11.codes_all
  1.7 0.7 reshape.12.codes_plane
  2.3 89.1 %shard_map.46 = f32[136,192]{1,0:T(8,128)} custom-call(s32[1,256]{1,0:T(1,128)} %reshape.11.codes_all, s32[4,1,64]{2,1,0:T(1,128)} %reshape.12.codes_plane, s32[4,4]{1,0:T(4,128)} %blocks.1, f32[4,16,4096]{2,1,0:T(8,128)} %amp.1, f32[1,1536,4096]{2,1,0:T(8,128)} %integ.1), custom_call_target="tpu_custom_call" | custom-call | flops 5133828096 | bytes 25165824 | tf_op jit(solution)/shard_map/pallas_call | solution.py:264
  91.4 2.0 %fusion = f32[256,192]{0,1:T(8,128)} fusion(f32[136,192]{1,0:T(8,128)} %shard_map.46, s32[256]{0:T(256)S(1)} %bitcast.4), kind=kOutput, calls=%fused_computation.1 | convolution fusion | flops 80250880 | bytes 302080 | tf_op jit(solution)/shard_map/dot_general | solution.py:300
  (1 shorter events, 0.0 us)

commit v2 on v1

v2 whole, which is shorter than its diff:
```python
import functools

import jax
import jax.numpy as jnp
from jax import lax
from jax.experimental import pallas as pl
from jax.experimental.pallas import tpu as pltpu
from jax.sharding import PartitionSpec as P

F32 = jnp.float32
BF16 = jnp.bfloat16
CHUNK = 128
GROUPS = 1
JOINT_LAG = 1
OUTER_LAG = 3
PRODUCT_LAG = 4
NT = (((1,), (1,)), ((), ()))
TN = (((0,), (0,)), ((), ()))


def split2(value):
    high = value.astype(BF16)
    return high, (value - high.astype(F32)).astype(BF16)


def dot(lhs, rhs):
    return jnp.dot(lhs, rhs, preferred_element_type=F32)


def ladder_kernel(
    nr, nc, nd,
    pair_list, block_list, amp, integ, out,
    pairs, blocks, slab, raw, joint, staged, chosen, acc, got_col, got_depth, mask_in, mask_ext, spread_back,
    pair_sem, block_sem, slab_sem, first_send, first_recv, line_send, line_recv, plane_send, plane_recv,
    col_send, col_recv, depth_send, depth_recv,
):
    r = lax.axis_index("row")
    c = lax.axis_index("col")
    d = lax.axis_index("depth")
    nblk, own_pairs, width = amp.shape
    quarter = width // nr
    steps = quarter // CHUNK
    plane_pairs = nr * own_pairs
    sym = mask_in.shape[0]
    share = out.shape[0]
    units = steps * GROUPS
    per_group = nblk // GROUPS

    def remote(src, dst, send, recv, **to):
        return pltpu.make_async_remote_copy(
            src_ref=src, dst_ref=dst, send_sem=send, recv_sem=recv,
            device_id=to, device_id_type=pl.DeviceIdType.MESH,
        )

    inner = jnp.logical_and(d >= 1, d <= 2)
    outer = jnp.logical_or(d == 0, d == 3)
    lower = d < 2
    ext = jnp.where(lower, 0, 3)
    mate = 3 - d
    inward = jnp.where(lower, d + 1, d - 1)
    outward = jnp.where(lower, 0, 3)

    barrier = pltpu.get_barrier_semaphore()
    for o in range(1, nr):
        pl.semaphore_signal(barrier, inc=1, device_id={"row": lax.rem(r + o, nr)},
                            device_id_type=pl.DeviceIdType.MESH)
    for o in range(1, nc):
        pl.semaphore_signal(barrier, inc=1, device_id={"col": lax.rem(c + o, nc)},
                            device_id_type=pl.DeviceIdType.MESH)
    for o in range(1, nd):
        pl.semaphore_signal(barrier, inc=1, device_id={"depth": lax.rem(d + o, nd)},
                            device_id_type=pl.DeviceIdType.MESH)
    slab_copy = pltpu.make_async_copy(integ.at[0], slab, slab_sem)
    pair_copy = pltpu.make_async_copy(pair_list, pairs, pair_sem)
    block_copy = pltpu.make_async_copy(block_list, blocks, block_sem)
    pair_copy.start()
    block_copy.start()
    pl.semaphore_wait(barrier, nr + nc + nd - 3)

    def first_copy(j, o):
        to = lax.rem(r + o, nr)
        at = pl.multiple_of(to * quarter + j * CHUNK, CHUNK)
        src = amp.at[:, :, pl.ds(at, CHUNK)]
        dst = raw.at[j, d, :, pl.ds(pl.multiple_of(r * own_pairs, own_pairs), own_pairs), :]
        if o == 0:
            return pltpu.make_async_copy(src, dst, first_recv.at[j, 0])
        return remote(src, dst, first_send.at[j, o], first_recv.at[j, o], row=to)

    def first_start(j, _):
        for o in range(nr):
            first_copy(j, o).start()
        return 0

    lax.fori_loop(0, 1, first_start, 0)

    pair_copy.wait()
    block_copy.wait()
    first, second = pairs[0:1, :], pairs[1:2, :]
    big, small = jnp.maximum(first, second), jnp.minimum(first, second)
    n = nd * plane_pairs
    hit = ((big * (big + 1)) >> 1) + small == lax.broadcasted_iota(jnp.int32, (n, n), 0)
    spread_back[...] = jnp.where(hit, 1.0, 0.0)[:sym]
    weighted = jnp.where(hit, jnp.where(big == small, 2.0, 1.0), 0.0).T
    planes = []
    for z in range(nd):
        planes.append(jnp.concatenate(
            [weighted[(q * nd + z) * own_pairs:(q * nd + z + 1) * own_pairs] for q in range(nr)], axis=0))
    none = jnp.zeros_like(planes[0])
    first_plane = jnp.where(lower, none, planes[0])
    last_plane = jnp.where(lower, planes[3], none)
    mask_in[...] = jnp.concatenate([first_plane, planes[1], planes[2], last_plane], axis=0).T[:sym]
    mask_ext[...] = jnp.concatenate([jnp.where(lower, planes[0], planes[3]), none], axis=0).T[:sym, :plane_pairs]
    acc[...] = jnp.zeros_like(acc)

    def part(ref, u, *at):
        return ref.at[(u // GROUPS, *at, pl.ds(lax.rem(u, GROUPS) * per_group, per_group))]

    def own_copy(u):
        return remote(part(raw, u, d), part(raw, u, d), line_send.at[u, 0], line_recv.at[u, d], depth=inward)

    def forward_copy(u):
        return remote(part(raw, u, outward), part(raw, u, outward), line_send.at[u, 1],
                      line_recv.at[u, outward], depth=inward)

    def joint_copy(u):
        return remote(part(joint, u), part(joint, u), line_send.at[u, 2], line_recv.at[u, nd], depth=outward)

    def raw_arrived(u, z):
        remote(part(raw, u, z), part(raw, u, z), line_send.at[u, 0], line_recv.at[u, z], depth=inward).wait_recv()

    def plane_copy(j, o):
        to = lax.rem(r + o, nr)
        return remote(staged.at[j, o], chosen.at[j, r], plane_send.at[j, o], plane_recv.at[j, o], row=to)

    def spread(j):
        m_ext = mask_ext[...].astype(BF16)
        sums = []
        for b in range(0, nblk, 2):
            high, low = split2(jnp.concatenate([raw[j, ext, b], raw[j, ext, b + 1]], axis=1))
            value = dot(m_ext, high) + dot(m_ext, low)
            sums.append(joint[j, b] + value[:, :CHUNK])
            sums.append(joint[j, b + 1] + value[:, CHUNK:])
        for o in range(nr):
            to = lax.rem(r + o, nr)
            at = lax.rem(jnp.maximum(blocks[d, to], 0), nblk)
            picked = sums[0]
            for b in range(1, nblk):
                picked = jnp.where(at == b, sums[b], picked)
            if o == 0:
                chosen[j, r] = picked
            else:
                staged[j, o] = picked
                plane_copy(j, o).start()

    def step(t, _):
        @pl.when(t + 1 < steps)
        def _():
            first_start(t + 1, 0)

        @pl.when(t == 1)
        def _():
            slab_copy.start()

        @pl.when(t < units)
        def _():
            @pl.when(lax.rem(t, GROUPS) == 0)
            def _():
                for o in range(nr):
                    copy = first_copy(t // GROUPS, o)
                    if o == 0:
                        copy.wait()
                    else:
                        copy.wait_recv()

            own_copy(t).start()

        @pl.when(jnp.logical_and(inner, t < units))
        def _():
            raw_arrived(t, outward)
            forward_copy(t).start()

        @pl.when(jnp.logical_and(inner, jnp.logical_and(t >= JOINT_LAG, t < units + JOINT_LAG)))
        def _():
            u = t - JOINT_LAG
            j = u // GROUPS
            raw_arrived(u, mate)
            raw_arrived(u, 3 - outward)
            m_in = mask_in[...].astype(BF16)
            for k in range(0, per_group, 2):
                b = lax.rem(u, GROUPS) * per_group + k
                high, low = split2(jnp.concatenate(
                    [raw[j, :, b + e].reshape(nd * plane_pairs, CHUNK) for e in range(2)], axis=1))
                value = dot(m_in, high) + dot(m_in, low)
                joint[j, b] = value[:, :CHUNK]
                joint[j, b + 1] = value[:, CHUNK:]
            joint_copy(u).start()

            @pl.when(lax.rem(u, GROUPS) == GROUPS - 1)
            def _():
                spread(j)

        @pl.when(jnp.logical_and(outer, jnp.logical_and(t >= OUTER_LAG, t < units + OUTER_LAG)))
        def _():
            u = t - OUTER_LAG
            joint_copy(u).wait_recv()

            @pl.when(lax.rem(u, GROUPS) == GROUPS - 1)
            def _():
                spread(u // GROUPS)

        @pl.when(t == PRODUCT_LAG)
        def _():
            slab_copy.wait()

        @pl.when(jnp.logical_and(t >= PRODUCT_LAG, lax.rem(t - PRODUCT_LAG, GROUPS) == GROUPS - 1))
        def _():
            j = (t - PRODUCT_LAG) // GROUPS
            for o in range(1, nr):
                plane_copy(j, o).wait_recv()
            lhs = jnp.concatenate([chosen[j, q] for q in range(nr)], axis=1)
            l_high = lhs.astype(BF16)
            l_both = jnp.concatenate([lhs, lhs - l_high.astype(F32)], axis=0).astype(BF16)

            def tile(s, _):
                rows = pl.ds(pl.multiple_of(s * share, 8), share)
                rhs = jnp.concatenate(
                    [slab[rows, pl.ds(pl.multiple_of(q * quarter + j * CHUNK, CHUNK), CHUNK)]
                     for q in range(nr)], axis=1)
                r_high, r_low = split2(rhs)
                both = lax.dot_general(l_both, r_high, NT, preferred_element_type=F32)
                value = lax.dot_general(l_high, r_low, NT, preferred_element_type=F32)
                value += both[:sym] + both[sym:]
                acc[s // nd, lax.rem(s, nd)] += value
                return 0

            lax.fori_loop(0, nc * nd, tile, 0)

        return 0

    lax.fori_loop(0, units + PRODUCT_LAG, step, 0)

    live = blocks[d, r] >= 0
    acc[...] = jnp.where(live, acc[...], 0.0)

    def col_copy(o):
        to = lax.rem(c + o, nc)
        return remote(acc.at[to], got_col.at[o], col_send.at[o], col_recv.at[o], col=to)

    for o in range(1, nc):
        col_copy(o).start()
    for o in range(1, nc):
        col_copy(o).wait_recv()
    total = acc[c]
    for o in range(1, nc):
        total += got_col[o]
    got_col[0] = total

    def depth_copy(o):
        to = lax.rem(d + o, nd)
        return remote(got_col.at[0, to], got_depth.at[o], depth_send.at[o], depth_recv.at[o], depth=to)

    for o in range(1, nd):
        depth_copy(o).start()
    for o in range(1, nd):
        depth_copy(o).wait_recv()
    total = got_col[0, d]
    for o in range(1, nd):
        total += got_depth[o]

    back = spread_back[...].astype(BF16)
    high, low = split2(total)
    out[...] = (lax.dot_general(high, back, TN, preferred_element_type=F32)
                + lax.dot_general(low, back, TN, preferred_element_type=F32))

    for o in range(1, nc):
        col_copy(o).wait_send()
    for o in range(1, nd):
        depth_copy(o).wait_send()

    def finish(j, _):
        for o in range(1, nr):
            first_copy(j, o).wait_send()
            plane_copy(j, o).wait_send()
        return 0

    lax.fori_loop(0, steps, finish, 0)

    def finish_line(u, _):
        own_copy(u).wait_send()

        @pl.when(inner)
        def _():
            forward_copy(u).wait_send()
            joint_copy(u).wait_send()

        return 0

    lax.fori_loop(0, units, finish_line, 0)


def per_device(mesh, integrals, amplitudes, block_list, pair_list):
    nr, nc, nd = mesh.shape["row"], mesh.shape["col"], mesh.shape["depth"]
    _, rows, width = integrals.shape
    nblk, own_pairs, _ = amplitudes.shape
    pairs = pair_list.shape[0]
    nocc = int(round(pairs ** 0.5))
    sym = nocc * (nocc + 1) // 2
    plane_pairs = nr * own_pairs
    share = rows // (nc * nd)
    steps = width // nr // CHUNK
    units = steps * GROUPS

    dma = pltpu.SemaphoreType.DMA
    return pl.pallas_call(
        functools.partial(ladder_kernel, nr, nc, nd),
        out_shape=jax.ShapeDtypeStruct((share, pairs), F32),
        in_specs=[
            pl.BlockSpec(memory_space=pl.ANY),
            pl.BlockSpec(memory_space=pl.ANY),
            pl.BlockSpec(memory_space=pl.ANY),
            pl.BlockSpec(memory_space=pl.ANY),
        ],
        out_specs=pl.BlockSpec(memory_space=pltpu.VMEM),
        scratch_shapes=[
            pltpu.VMEM((2, pairs), jnp.int32),
            pltpu.SMEM(block_list.shape, jnp.int32),
            pltpu.VMEM((rows, width), F32),
            pltpu.VMEM((steps, nd, nblk, plane_pairs, CHUNK), F32),
            pltpu.VMEM((steps, nblk, sym, CHUNK), F32),
            pltpu.VMEM((steps, nr, sym, CHUNK), F32),
            pltpu.VMEM((steps, nr, sym, CHUNK), F32),
            pltpu.VMEM((nc, nd, sym, share), F32),
            pltpu.VMEM((nc, nd, sym, share), F32),
            pltpu.VMEM((nd, sym, share), F32),
            pltpu.VMEM((sym, pairs), F32),
            pltpu.VMEM((sym, plane_pairs), F32),
            pltpu.VMEM((sym, pairs), F32),
            dma, dma, dma, dma((steps, nr)), dma((steps, nr)),
            dma((units, 3)), dma((units, nd + 1)),
            dma((steps, nr)), dma((steps, nr)),
            dma((nc,)), dma((nc,)), dma((nd,)), dma((nd,)),
        ],
        compiler_params=pltpu.CompilerParams(
            collective_id=0, has_side_effects=True, vmem_limit_bytes=56 * 1024 * 1024
        ),
        cost_estimate=pl.CostEstimate(
            flops=6 * sym * rows * width, bytes_accessed=4 * rows * width, transcendentals=0
        ),
    )(pair_list.T, block_list, amplitudes, integrals).T


def solution(mesh):
    return jax.shard_map(
        functools.partial(per_device, mesh),
        mesh=mesh,
        in_specs=(
            P(("col", "depth"), "row", None),
            P("col", ("row", "depth"), None),
            P("col", None),
            P(),
        ),
        out_specs=P(None, ("row", "col", "depth")),
        check_vma=False,
    )
```

time: 93.6 us -> 86.4 us (0.923)
  Pallas kernels: 89.1 us -> 84.6 us
  matrix products: 1.99 us -> 0 us
    pallas_call x1, Pallas kernels: 89.1 us -> 84.6 us  [per_device(): pl.pallas_call(functools.partial(ladder_kernel, nr, nc, nd), out_shape=ja...]
    dot_general x1 -> x0, matrix products: 1.99 us -> none  [per_device(): jnp.dot(expand, sums, precision=lax.Precision.HIGHEST, preferred_element_...]
    unnamed x0 -> x1, local copies, waits for them, and re-layouts: none -> 1.62 us
    reshape x2 -> x0, local copies, waits for them, and re-layouts: 1.33 us -> none  [the longest x1 0.67 us: per_device(): codes_all = codes.reshape(1, pairs)]
where the time goes in v2:
time: 86.4 us; the launch traced here: 86.2 us
  Pallas kernels  84.6 us (98%)
  local copies, waits for them, and re-layouts  1.62 us (2%)
    pallas_call x1, Pallas kernels, per_device(): pl.pallas_call(functools.partial(ladder_kernel, nr, nc, nd), out_shape=ja...  84.6 us

profile of v2, /device:TPU:1, one launch (start us, length us, event | category | flops | bytes accessed | tf_op | source)
XLA Modules:
  0.0 86.2 jit_solution(3531856979503395841)
XLA Ops:
  0.0 84.6 %shard_map.46 = f32[192,256]{1,0:T(8,128)} custom-call(s32[2,256]{1,0:T(2,128)} %bitcast.3, s32[4,4]{1,0:T(4,128)} %block_list.1, f32[4,16,4096]{2,1,0:T(8,128)} %amp.1, f32[1,1536,4096]{2,1,0:T(8,128)} %integ.1), custom_call_target="tpu_custom_call" | custom-call | flops 5133828096 | bytes 25165824 | tf_op jit(solution)/shard_map/pallas_call | solution.py:314
  84.6 1.6 %copy.6 = f32[256,192]{0,1:T(8,128)} copy(f32[256,192]{0,1:T(8,128)} %bitcast.2) | data formatting | bytes 393216

commit v3 on v2

--- a/solution.py
+++ b/solution.py
@@ -233,7 +233,7 @@
                 acc[s // nd, lax.rem(s, nd)] += value
                 return 0
 
-            lax.fori_loop(0, nc * nd, tile, 0)
+            lax.fori_loop(0, nc * nd, tile, 0, unroll=min(4, nc * nd))
 
         return 0
 

time: 86.4 us -> 85 us (0.984)
  Pallas kernels: 84.6 us -> 83.2 us
    pallas_call x1, Pallas kernels: 84.6 us -> 83.2 us  [per_device(): pl.pallas_call(functools.partial(ladder_kernel, nr, nc, nd), out_shape=ja...]
where the time goes in v3:
time: 85 us; the launch traced here: 84.8 us
  Pallas kernels  83.2 us (98%)
  local copies, waits for them, and re-layouts  1.62 us (2%)
    pallas_call x1, Pallas kernels, per_device(): pl.pallas_call(functools.partial(ladder_kernel, nr, nc, nd), out_shape=ja...  83.2 us

profile of v3, /device:TPU:1, one launch (start us, length us, event | category | flops | bytes accessed | tf_op | source)
XLA Modules:
  0.0 84.8 jit_solution(284657373010828062)
XLA Ops:
  0.0 83.2 %shard_map.46 = f32[192,256]{1,0:T(8,128)} custom-call(s32[2,256]{1,0:T(2,128)} %bitcast.3, s32[4,4]{1,0:T(4,128)} %block_list.1, f32[4,16,4096]{2,1,0:T(8,128)} %amp.1, f32[1,1536,4096]{2,1,0:T(8,128)} %integ.1), custom_call_target="tpu_custom_call" | custom-call | flops 5133828096 | bytes 25165824 | tf_op jit(solution)/shard_map/pallas_call | solution.py:314
  83.2 1.6 %copy.6 = f32[256,192]{0,1:T(8,128)} copy(f32[256,192]{0,1:T(8,128)} %bitcast.2) | data formatting | bytes 393216
